TPU v7x, 32 devices: a whole 2x2x4 slice. The times are simulated.
32 devices in a mesh: dp: 8 (over z, x), walk: 4 (over y, core).
Axes of the slice: x: 2, y: 2, z: 4, core: 2. Of those that a mesh axis runs over, the one named last changes fastest.
Arguments:
- fields: float32 [512, 65536], P('walk', 'dp'), may hold values from -6 to 6
- sensitivity: bfloat16 [256, 16, 128, 128], P('dp'), may hold values from -0.125 to 0.125
- tile_index: int32 [256, 16], P('dp'), may hold values from 0 to 511
- tile_count: int32 [256], P('dp'), may hold values from 1 to 16, as said below
- observed: float32 [32768], P('dp'), may hold values from -6 to 6
- precision: float32 [32768], P('dp'), may hold values from 0.2 to 4
Outputs:
- fields_next: float32 [512, 65536], P('walk', 'dp')
Inputs may be any that keep to these rules, and one draw needn't show every extreme that they name: `tile_count`: every block of rows uses between 1 and 16 slots, and some block uses all 16; slots at or past the count are ignored.
All inputs are finite; a program needn't handle non-finite values.
Results may differ from a plain program's by a relative error of at most 0.0023.
Values may be sent and summed in bfloat16 or wider, within the bound.
A program may use at most 128 MiB of HBM per device.

v0:
```python
import jax
import jax.numpy as jnp
from jax import lax
from jax.sharding import PartitionSpec as P

WALKERS = 512


def forward(gathered, sensitivity, tile_index, tile_count):
    walkers_here = gathered.shape[0]
    nblocks = sensitivity.shape[0]
    tile_rows = sensitivity.shape[2]
    cell_blocks = gathered.reshape(walkers_here, -1, tile_rows)
    most_live = jnp.max(tile_count)

    def one_slot(slot_id, totals):
        columns = lax.dynamic_index_in_dim(tile_index, slot_id, 1, keepdims=False)
        blocks = jnp.take(cell_blocks, columns, axis=1)
        sensitive = lax.dynamic_index_in_dim(sensitivity, slot_id, 1, keepdims=False)
        product = jnp.einsum("brc,wbc->wbr", sensitive, blocks, preferred_element_type=jnp.float32)
        alive_mask = (slot_id < tile_count)[None, :, None]
        return totals + jnp.where(alive_mask, product, jnp.float32(0.0))

    start_sum = jnp.zeros((walkers_here, nblocks, tile_rows), jnp.float32)
    totals = lax.fori_loop(0, most_live, one_slot, start_sum)
    return totals.reshape(walkers_here, nblocks * tile_rows)


def local(fields, sensitivity, tile_index, tile_count, observed, precision):
    field_bf = fields.astype(jnp.bfloat16)
    gathered = lax.all_gather(field_bf, "dp", axis=1, tiled=True)
    predicted = forward(gathered, sensitivity, tile_index, tile_count)
    pred_sum = lax.psum(jnp.sum(predicted, axis=0), "walk")
    pred_mean = pred_sum / WALKERS
    deviation = (predicted - pred_mean[None, :]).astype(jnp.bfloat16)
    misfit = (precision[None, :] * (predicted - observed[None, :])).astype(jnp.bfloat16)
    partial_rows = lax.dot_general(
        misfit,
        lax.all_gather(deviation, "walk", axis=0, tiled=True),
        (((1,), (1,)), ((), ())),
        preferred_element_type=jnp.float32,
    )
    coupling_mine = lax.psum(partial_rows, "dp") / WALKERS
    squares = lax.psum(jnp.sum(coupling_mine * coupling_mine), "walk")
    spread = jnp.sqrt(squares / (WALKERS * WALKERS) + 1e-06)
    weights = (8.0 * coupling_mine / (WALKERS * spread)).astype(jnp.bfloat16)
    update = jnp.dot(
        weights,
        lax.all_gather(field_bf, "walk", axis=0, tiled=True),
        preferred_element_type=jnp.float32,
    )
    return fields - update


def solution(mesh):
    placed = (P("walk", "dp"), P("dp", None, None, None), P("dp", None), P("dp"), P("dp"), P("dp"))
    return jax.shard_map(
        local, mesh=mesh, in_specs=placed, out_specs=P("walk", "dp"), check_vma=False
    )
```

profile of v0, /device:TPU:0, one launch (start us, length us, event | category | flops | bytes accessed | tf_op | source)
XLA Modules:
  0.0 632.2 jit_solution(5999888927857076047)
XLA Ops:
  11.9 229.7 %all-gather.4.cloned.1.call-done = bf16[128,65536]{0,1:T(8,128)(2,1)} async-done(((bf16[128,8192]{0,1:T(8,128)(2,1)}), bf16[128,65536]{0,1:T(8,128)(2,1)}) %all-gather.4.cloned.1.call-update) | async-done | bytes 16777232 | tf_op jit(solution)/shard_map/all_gather | solution.py:31
  241.7 22.4 %copy.12 = bf16[128,512,128]{2,0,1:T(8,128)(2,1)} copy(bf16[128,512,128]{0,2,1:T(8,128)(2,1)} %bitcast.37) | data formatting | bytes 33554432 | tf_op jit(solution)/shard_map/while | solution.py:25
  264.3 167.2 %while.10 = (s32[]{:T(128)}, f32[128,32,128]{2,0,1:T(8,128)S(1)}, s32[]{:T(128)}, s32[32]{0:T(128)S(1)}, s32[32,16]{0,1:T(8,128)}, /*index=5*/bf16[128,512,128]{...) while((s32[]{:T(128)}, f32[128,32,128]{2,0,1:T(8,128)S(1)}, ...), condition=%wide.region_2.3_spmd, body=%wide.region_1.2_spmd.sunk | while | flops 135791840 | bytes 8393619 | solution.py:25
  265.6 6.5 %gather_fusion = bf16[32,128,128]{2,1,0:T(8,128)(2,1)S(1)} fusion(bf16[128,512,128]{2,0,1:T(8,128)(2,1)} %get-tuple-element.156, s32[1024]{0:T(1024)S(1)} %pad_clamp_fusion.2), kind=kCustom, calls=%fused_computation.clone.1 | custom fusion | bytes 2097280 | tf_op jit(solution)/shard_map/while/body/jit(_take)/gather | solution.py:18
  276.1 6.5 %gather_fusion = bf16[32,128,128]{2,1,0:T(8,128)(2,1)S(1)} fusion(bf16[128,512,128]{2,0,1:T(8,128)(2,1)} %get-tuple-element.156, s32[1024]{0:T(1024)S(1)} %pad_clamp_fusion.2), kind=kCustom, calls=%fused_computation.clone.1 | custom fusion | bytes 2097280 | tf_op jit(solution)/shard_map/while/body/jit(_take)/gather | solution.py:18
  286.5 6.5 %gather_fusion = bf16[32,128,128]{2,1,0:T(8,128)(2,1)S(1)} fusion(bf16[128,512,128]{2,0,1:T(8,128)(2,1)} %get-tuple-element.156, s32[1024]{0:T(1024)S(1)} %pad_clamp_fusion.2), kind=kCustom, calls=%fused_computation.clone.1 | custom fusion | bytes 2097280 | tf_op jit(solution)/shard_map/while/body/jit(_take)/gather | solution.py:18
  296.9 6.5 %gather_fusion = bf16[32,128,128]{2,1,0:T(8,128)(2,1)S(1)} fusion(bf16[128,512,128]{2,0,1:T(8,128)(2,1)} %get-tuple-element.156, s32[1024]{0:T(1024)S(1)} %pad_clamp_fusion.2), kind=kCustom, calls=%fused_computation.clone.1 | custom fusion | bytes 2097280 | tf_op jit(solution)/shard_map/while/body/jit(_take)/gather | solution.py:18
  307.3 6.5 %gather_fusion = bf16[32,128,128]{2,1,0:T(8,128)(2,1)S(1)} fusion(bf16[128,512,128]{2,0,1:T(8,128)(2,1)} %get-tuple-element.156, s32[1024]{0:T(1024)S(1)} %pad_clamp_fusion.2), kind=kCustom, calls=%fused_computation.clone.1 | custom fusion | bytes 2097280 | tf_op jit(solution)/shard_map/while/body/jit(_take)/gather | solution.py:18
  317.7 6.5 %gather_fusion = bf16[32,128,128]{2,1,0:T(8,128)(2,1)S(1)} fusion(bf16[128,512,128]{2,0,1:T(8,128)(2,1)} %get-tuple-element.156, s32[1024]{0:T(1024)S(1)} %pad_clamp_fusion.2), kind=kCustom, calls=%fused_computation.clone.1 | custom fusion | bytes 2097280 | tf_op jit(solution)/shard_map/while/body/jit(_take)/gather | solution.py:18
  328.1 6.5 %gather_fusion = bf16[32,128,128]{2,1,0:T(8,128)(2,1)S(1)} fusion(bf16[128,512,128]{2,0,1:T(8,128)(2,1)} %get-tuple-element.156, s32[1024]{0:T(1024)S(1)} %pad_clamp_fusion.2), kind=kCustom, calls=%fused_computation.clone.1 | custom fusion | bytes 2097280 | tf_op jit(solution)/shard_map/while/body/jit(_take)/gather | solution.py:18
  338.5 6.5 %gather_fusion = bf16[32,128,128]{2,1,0:T(8,128)(2,1)S(1)} fusion(bf16[128,512,128]{2,0,1:T(8,128)(2,1)} %get-tuple-element.156, s32[1024]{0:T(1024)S(1)} %pad_clamp_fusion.2), kind=kCustom, calls=%fused_computation.clone.1 | custom fusion | bytes 2097280 | tf_op jit(solution)/shard_map/while/body/jit(_take)/gather | solution.py:18
  348.9 6.5 %gather_fusion = bf16[32,128,128]{2,1,0:T(8,128)(2,1)S(1)} fusion(bf16[128,512,128]{2,0,1:T(8,128)(2,1)} %get-tuple-element.156, s32[1024]{0:T(1024)S(1)} %pad_clamp_fusion.2), kind=kCustom, calls=%fused_computation.clone.1 | custom fusion | bytes 2097280 | tf_op jit(solution)/shard_map/while/body/jit(_take)/gather | solution.py:18
  359.3 6.5 %gather_fusion = bf16[32,128,128]{2,1,0:T(8,128)(2,1)S(1)} fusion(bf16[128,512,128]{2,0,1:T(8,128)(2,1)} %get-tuple-element.156, s32[1024]{0:T(1024)S(1)} %pad_clamp_fusion.2), kind=kCustom, calls=%fused_computation.clone.1 | custom fusion | bytes 2097280 | tf_op jit(solution)/shard_map/while/body/jit(_take)/gather | solution.py:18
  369.7 6.5 %gather_fusion = bf16[32,128,128]{2,1,0:T(8,128)(2,1)S(1)} fusion(bf16[128,512,128]{2,0,1:T(8,128)(2,1)} %get-tuple-element.156, s32[1024]{0:T(1024)S(1)} %pad_clamp_fusion.2), kind=kCustom, calls=%fused_computation.clone.1 | custom fusion | bytes 2097280 | tf_op jit(solution)/shard_map/while/body/jit(_take)/gather | solution.py:18
  380.1 6.5 %gather_fusion = bf16[32,128,128]{2,1,0:T(8,128)(2,1)S(1)} fusion(bf16[128,512,128]{2,0,1:T(8,128)(2,1)} %get-tuple-element.156, s32[1024]{0:T(1024)S(1)} %pad_clamp_fusion.2), kind=kCustom, calls=%fused_computation.clone.1 | custom fusion | bytes 2097280 | tf_op jit(solution)/shard_map/while/body/jit(_take)/gather | solution.py:18
  390.5 6.5 %gather_fusion = bf16[32,128,128]{2,1,0:T(8,128)(2,1)S(1)} fusion(bf16[128,512,128]{2,0,1:T(8,128)(2,1)} %get-tuple-element.156, s32[1024]{0:T(1024)S(1)} %pad_clamp_fusion.2), kind=kCustom, calls=%fused_computation.clone.1 | custom fusion | bytes 2097280 | tf_op jit(solution)/shard_map/while/body/jit(_take)/gather | solution.py:18
  401.0 6.5 %gather_fusion = bf16[32,128,128]{2,1,0:T(8,128)(2,1)S(1)} fusion(bf16[128,512,128]{2,0,1:T(8,128)(2,1)} %get-tuple-element.156, s32[1024]{0:T(1024)S(1)} %pad_clamp_fusion.2), kind=kCustom, calls=%fused_computation.clone.1 | custom fusion | bytes 2097280 | tf_op jit(solution)/shard_map/while/body/jit(_take)/gather | solution.py:18
  411.4 6.5 %gather_fusion = bf16[32,128,128]{2,1,0:T(8,128)(2,1)S(1)} fusion(bf16[128,512,128]{2,0,1:T(8,128)(2,1)} %get-tuple-element.156, s32[1024]{0:T(1024)S(1)} %pad_clamp_fusion.2), kind=kCustom, calls=%fused_computation.clone.1 | custom fusion | bytes 2097280 | tf_op jit(solution)/shard_map/while/body/jit(_take)/gather | solution.py:18
  421.8 6.5 %gather_fusion = bf16[32,128,128]{2,1,0:T(8,128)(2,1)S(1)} fusion(bf16[128,512,128]{2,0,1:T(8,128)(2,1)} %get-tuple-element.156, s32[1024]{0:T(1024)S(1)} %pad_clamp_fusion.2), kind=kCustom, calls=%fused_computation.clone.1 | custom fusion | bytes 2097280 | tf_op jit(solution)/shard_map/while/body/jit(_take)/gather | solution.py:18
  433.5 10.5 %psum.21 = f32[4096]{0:T(1024)S(1)} all-reduce(f32[4096]{0:T(1024)S(1)} %bitcast.38), channel_id=1, replica_groups=mesh['dp'=8,'walk'=4] {'walk'}, use_global_device_ids=true, to_apply=%region_4.5 | all-reduce | flops 4096 | bytes 32768 | tf_op jit(solution)/shard_map/psum | solution.py:33
  448.5 33.1 %all-gather.6.cloned.1.call-done = bf16[512,4096]{0,1:T(8,128)(2,1)} async-done(((bf16[128,4096]{0,1:T(8,128)(2,1)}), bf16[512,4096]{0,1:T(8,128)(2,1)}) %all-gather.6.cloned.1.call-update) | async-done | bytes 4194320 | tf_op jit(solution)/shard_map/all_gather | solution.py:39
  485.8 70.1 %all-reduce.2.cloned.1.call-done = f32[128,512]{1,0:T(8,128)} async-done(((f32[128,512]{1,0:T(8,128)}), f32[128,512]{1,0:T(8,128)}) %all-reduce.2.cloned.1.call-update) | async-done | bytes 262160 | tf_op jit(solution)/shard_map/psum | solution.py:43
  564.5 51.7 %all-gather.8.cloned.1.call-done = bf16[512,8192]{0,1:T(8,128)(2,1)} async-done(((bf16[128,8192]{0,1:T(8,128)(2,1)}), bf16[512,8192]{0,1:T(8,128)(2,1)}) %all-gather.8.cloned.1.call-update) | async-done | bytes 8388624 | tf_op jit(solution)/shard_map/all_gather | solution.py:49
  616.2 9.5 %convolution_subtract_fusion = f32[128,8192]{1,0:T(8,128)} fusion(f32[128,8192]{1,0:T(8,128)} %param.8, bf16[512,8192]{0,1:T(8,128)(2,1)} %all-gather.8.cloned.1.call-done, f32[128,512]{1,0:T(8,128)} %all-reduce.2.cloned.1.call-done, f32[]{:T(128)S(6)} %mul.25), kind=kOutput, calls=%fused_computation.14 | convolution fusion | flops 1074987008 | bytes 17039364 | tf_op jit(solution)/shard_map/dot_general | solution.py:47
  (88 shorter events, 76.1 us)
Async XLA Ops:
  6.5 4.7 copy-start.2
  6.5 235.1 %all-gather.4.cloned.1.call-start = ((), (), s32[]{:S(2)}) async-start(), calls=%async_computation | async-start | bytes 18874368 | tf_op jit(solution)/shard_map/all_gather | solution.py:31
  11.2 470.4 %all-gather.6.cloned.1.call-start = ((), (), s32[]{:S(2)}) async-start(), calls=%async_computation.1 | async-start | bytes 5242880 | tf_op jit(solution)/shard_map/all_gather | solution.py:39
  431.5 12.5 %copy-start = (f32[4096]{0:T(1024)S(1)}, f32[4096]{0:T(1024)}, u32[]{:S(2)}) copy-start(f32[4096]{0:T(1024)} %param.12) | copy-start | bytes 49156
  431.5 12.5 %copy-start.1 = (f32[4096]{0:T(1024)S(1)}, f32[4096]{0:T(1024)}, u32[]{:S(2)}) copy-start(f32[4096]{0:T(1024)} %param.13) | copy-start | bytes 49156
  448.5 107.5 %all-reduce.2.cloned.1.call-start = ((), (), s32[]{:S(2)}) async-start(), calls=%async_computation.2 | async-start | bytes 524288 | tf_op jit(solution)/shard_map/psum | solution.py:43
  485.3 130.9 %all-gather.8.cloned.1.call-start = ((), (), s32[]{:S(2)}) async-start(), calls=%async_computation.3 | async-start | bytes 10485760 | tf_op jit(solution)/shard_map/all_gather | solution.py:49
Sparse Core Ops, SparseCore 0:
  11.3 230.2 all-gather.3
  448.6 32.9 all-gather.5
  485.4 70.5 all-reduce.1
  557.5 58.6 all-gather.7
where the time goes:
time: 635 us; the launch traced here: 632 us
  waiting for transfers between devices  385 us (61%)
  local copies, waits for them, and re-layouts  133 us (21%)
  matrix products  53.6 us (8%)
  other arithmetic  18.3 us (3%)
  blocking collectives  16.7 us (3%)
  between operations  13.8 us (2%)
  loops' own time  11 us (2%)
    all_gather x1, waiting for transfers between devices, local(): gathered = lax.all_gather(field_bf, 'dp', axis=1, tiled=True)  230 us
    gather x16, local copies, waits for them, and re-layouts, one_slot(): blocks = jnp.take(cell_blocks, columns, axis=1)  104 us
    psum x1, waiting for transfers between devices, local(): coupling_mine = lax.psum(partial_rows, 'dp') / WALKERS  70.1 us
    all_gather x1, waiting for transfers between devices, local(): lax.all_gather(field_bf, 'walk', axis=0, tiled=True)  51.7 us
    dot_general x16, matrix products, one_slot(): jnp.einsum('brc,wbc->wbr', sensitive, blocks, preferred_element_type=jnp....  40.4 us
    all_gather x1, waiting for transfers between devices, local(): lax.all_gather(deviation, 'walk', axis=0, tiled=True)  33.1 us
    while x2, local copies, waits for them, and re-layouts, forward(): totals = lax.fori_loop(0, most_live, one_slot, start_sum)  24.3 us
  transfers between devices with their start and end apart: 4, of which 4 were waited for; matrix products, arithmetic and copies ran while one was open for 0% of the time, Pallas kernels for 0%

commit v1 on v0

--- a/solution.py
+++ b/solution.py
@@ -28,7 +28,22 @@
 
 def local(fields, sensitivity, tile_index, tile_count, observed, precision):
     field_bf = fields.astype(jnp.bfloat16)
-    gathered = lax.all_gather(field_bf, "dp", axis=1, tiled=True)
+    ways, here, step = (lax.axis_size("dp"), lax.axis_index("dp"), field_bf.shape[1])
+    dims = [n * ways if d == 1 else n for d, n in enumerate(field_bf.shape)]
+    gathered = lax.dynamic_update_slice_in_dim(
+        jnp.zeros(dims, field_bf.dtype), field_bf, here * step, axis=1
+    )
+    going_up = going_down = field_bf
+    for far in range(1, ways // 2 + 1):
+        going_up = lax.ppermute(going_up, "dp", [(d, (d + 1) % ways) for d in range(ways)])
+        gathered = lax.dynamic_update_slice_in_dim(
+            gathered, going_up, (here - far) % ways * step, axis=1
+        )
+        if 2 * far < ways:
+            going_down = lax.ppermute(going_down, "dp", [(d, (d - 1) % ways) for d in range(ways)])
+            gathered = lax.dynamic_update_slice_in_dim(
+                gathered, going_down, (here + far) % ways * step, axis=1
+            )
     predicted = forward(gathered, sensitivity, tile_index, tile_count)
     pred_sum = lax.psum(jnp.sum(predicted, axis=0), "walk")
     pred_mean = pred_sum / WALKERS

time: 635 us -> 729 us (1.15)
  waiting for transfers between devices: 385 us -> 436 us
  local copies, waits for them, and re-layouts: 133 us -> 157 us
  starting transfers between devices: 0.13 us -> 19.8 us
    ppermute x0 -> x7, waiting for transfers between devices: none -> 283 us  [the longest x4 241 us: local(): lax.ppermute(going_up, 'dp', [(d, (d + 1) % ways) for d in range(ways)])]
    all_gather x1 -> x0, waiting for transfers between devices: 230 us -> none  [local(): gathered = lax.all_gather(field_bf, 'dp', axis=1, tiled=True)]
    ppermute x0 -> x7, starting transfers between devices: none -> 19.7 us  [the longest x4 10.4 us: local(): lax.ppermute(going_up, 'dp', [(d, (d + 1) % ways) for d in range(ways)])]
    dynamic_update_slice x0 -> x8, local copies, waits for them, and re-layouts: none -> 18.1 us  [the longest x4 9.04 us: local(): lax.dynamic_update_slice_in_dim(gathered, going_up, (here - far) % ways *...]
  transfers between devices with their start and end apart: 4 -> 10, of which waited for: 4 -> 7; matrix products, arithmetic and copies ran while one was open for 0% -> 3% of each run, Pallas kernels for 0% -> 0%
where the time goes in v1:
time: 729 us; the launch traced here: 726 us
  waiting for transfers between devices  436 us (60%)
  local copies, waits for them, and re-layouts  157 us (22%)
  matrix products  53.6 us (7%)
  starting transfers between devices  19.8 us (3%)
  other arithmetic  18.3 us (3%)
  blocking collectives  17.5 us (2%)
  between operations  13.9 us (2%)
  loops' own time  9.94 us (1%)
    ppermute x4, waiting for transfers between devices, local(): lax.ppermute(going_up, 'dp', [(d, (d + 1) % ways) for d in range(ways)])  241 us
    gather x16, local copies, waits for them, and re-layouts, one_slot(): blocks = jnp.take(cell_blocks, columns, axis=1)  104 us
    psum x1, waiting for transfers between devices, local(): coupling_mine = lax.psum(partial_rows, 'dp') / WALKERS  70 us
    all_gather x1, waiting for transfers between devices, local(): lax.all_gather(field_bf, 'walk', axis=0, tiled=True)  51.6 us
    ppermute x3, waiting for transfers between devices, local(): lax.ppermute(going_down, 'dp', [(d, (d - 1) % ways) for d in range(ways)])  41.5 us
    dot_general x16, matrix products, one_slot(): jnp.einsum('brc,wbc->wbr', sensitive, blocks, preferred_element_type=jnp....  40.5 us
    all_gather x1, waiting for transfers between devices, local(): lax.all_gather(deviation, 'walk', axis=0, tiled=True)  31.4 us
    while x2, local copies, waits for them, and re-layouts, forward(): totals = lax.fori_loop(0, most_live, one_slot, start_sum)  24.2 us
  transfers between devices with their start and end apart: 10, of which 7 were waited for; matrix products, arithmetic and copies ran while one was open for 3% of the time, Pallas kernels for 0%

profile of v1, /device:TPU:0, one launch (start us, length us, event | category | flops | bytes accessed | tf_op | source)
XLA Modules:
  0.0 726.0 jit_solution(16193383449347906237)
XLA Ops:
  16.3 86.7 %collective-permute-done = bf16[128,8192]{0,1:T(8,128)(2,1)} collective-permute-done((bf16[128,8192]{0,1:T(8,128)(2,1)S(1)}, bf16[128,8192]{0,1:T(8,128)(2,1)}, u32[]{:S(2)}, u32[]{:S(2)}) %collective-permute-start) | collective-permute-done | bytes 2097184 | tf_op jit(solution)/shard_map/ppermute | solution.py:38
  116.8 78.2 %collective-permute-done.2 = bf16[128,8192]{0,1:T(8,128)(2,1)} collective-permute-done((bf16[128,8192]{0,1:T(8,128)(2,1)}, bf16[128,8192]{0,1:T(8,128)(2,1)}, u32[]{:S(2)}, u32[]{:S(2)}) %collective-permute-start.2) | collective-permute-done | bytes 2097184 | tf_op jit(solution)/shard_map/ppermute | solution.py:38
  209.6 76.3 %collective-permute-done.4 = bf16[128,8192]{0,1:T(8,128)(2,1)S(1)} collective-permute-done((bf16[128,8192]{0,1:T(8,128)(2,1)}, bf16[128,8192]{0,1:T(8,128)(2,1)S(1)}, u32[]{:S(2)}, u32[]{:S(2)}) %collective-permute-start.4) | collective-permute-done | bytes 2097184 | tf_op jit(solution)/shard_map/ppermute | solution.py:38
  292.9 41.5 %collective-permute-done.5 = bf16[128,8192]{0,1:T(8,128)(2,1)S(1)} collective-permute-done((bf16[128,8192]{0,1:T(8,128)(2,1)}, bf16[128,8192]{0,1:T(8,128)(2,1)S(1)}, u32[]{:S(2)}, u32[]{:S(2)}) %collective-permute-start.5) | collective-permute-done | bytes 2097184 | tf_op jit(solution)/shard_map/ppermute | solution.py:43
  337.4 22.4 %copy.12 = bf16[128,512,128]{2,0,1:T(8,128)(2,1)} copy(bf16[128,512,128]{0,2,1:T(8,128)(2,1)} %bitcast.5) | data formatting | bytes 33554432 | tf_op jit(solution)/shard_map/while | solution.py:25
  360.0 166.1 %while.10 = (s32[]{:T(128)}, f32[128,32,128]{2,0,1:T(8,128)S(1)}, s32[]{:T(128)}, s32[32]{0:T(128)S(1)}, s32[32,16]{0,1:T(8,128)}, /*index=5*/bf16[128,512,128]{...) while((s32[]{:T(128)}, f32[128,32,128]{2,0,1:T(8,128)S(1)}, ...), condition=%wide.region_2.3_spmd, body=%wide.region_1.2_spmd.sunk | while | flops 135791840 | bytes 8393619 | solution.py:25
  361.2 6.5 gather_fusion
  371.6 6.5 gather_fusion
  381.9 6.5 gather_fusion
  392.3 6.5 gather_fusion
  402.6 6.5 gather_fusion
  423.3 6.5 gather_fusion
  433.7 6.5 gather_fusion
  444.0 6.5 gather_fusion
  454.4 6.5 gather_fusion
  464.7 6.5 gather_fusion
  475.1 6.5 gather_fusion
  495.8 6.5 gather_fusion
  506.1 6.5 gather_fusion
  528.1 11.2 %psum.21 = f32[4096]{0:T(1024)S(1)} all-reduce(f32[4096]{0:T(1024)S(1)} %bitcast.37), channel_id=1, replica_groups=mesh['dp'=8,'walk'=4] {'walk'}, use_global_device_ids=true, to_apply=%region_4.5 | all-reduce | flops 4096 | bytes 32768 | tf_op jit(solution)/shard_map/psum | solution.py:48
  543.9 31.4 %all-gather.3.cloned.1.call-done = bf16[512,4096]{0,1:T(8,128)(2,1)} async-done(((bf16[128,4096]{0,1:T(8,128)(2,1)}), bf16[512,4096]{0,1:T(8,128)(2,1)}) %all-gather.3.cloned.1.call-update) | async-done | bytes 4194320 | tf_op jit(solution)/shard_map/all_gather | solution.py:54
  579.7 70.0 %all-reduce.2.cloned.1.call-done = f32[128,512]{1,0:T(8,128)} async-done(((f32[128,512]{1,0:T(8,128)}), f32[128,512]{1,0:T(8,128)}) %all-reduce.2.cloned.1.call-update) | async-done | bytes 262160 | tf_op jit(solution)/shard_map/psum | solution.py:58
  658.4 51.6 %all-gather.5.cloned.1.call-done = bf16[512,8192]{0,1:T(8,128)(2,1)} async-done(((bf16[128,8192]{0,1:T(8,128)(2,1)}), bf16[512,8192]{0,1:T(8,128)(2,1)}) %all-gather.5.cloned.1.call-update) | async-done | bytes 8388624 | tf_op jit(solution)/shard_map/all_gather | solution.py:64
  710.0 9.5 %convolution_subtract_fusion = f32[128,8192]{1,0:T(8,128)} fusion(f32[128,8192]{1,0:T(8,128)} %param.8, bf16[512,8192]{0,1:T(8,128)(2,1)} %all-gather.5.cloned.1.call-done, f32[128,512]{1,0:T(8,128)} %all-reduce.2.cloned.1.call-done, f32[]{:T(128)S(6)} %mul.57), kind=kOutput, calls=%fused_computation.14 | convolution fusion | flops 1074987008 | bytes 17039364 | tf_op jit(solution)/shard_map/dot_general | solution.py:62
  (110 shorter events, 138.7 us)
Async XLA Ops:
  6.5 568.8 %all-gather.3.cloned.1.call-start = ((), (), s32[]{:S(2)}) async-start(), calls=%async_computation | async-start | bytes 5242880 | tf_op jit(solution)/shard_map/all_gather | solution.py:54
  10.2 104.5 %copy-start = (bf16[128,8192]{0,1:T(8,128)(2,1)}, bf16[128,8192]{0,1:T(8,128)(2,1)S(1)}, u32[]{:S(2)}) copy-start(bf16[128,8192]{0,1:T(8,128)(2,1)S(1)} %copy.11) | copy-start | bytes 6291460
  10.3 92.8 %collective-permute-start = (bf16[128,8192]{0,1:T(8,128)(2,1)S(1)}, bf16[128,8192]{0,1:T(8,128)(2,1)}, u32[]{:S(2)}, u32[]{:S(2)}) collective-permute-start(bf16[128,8192]{0,1:T(8,128)(2,1)S(1)} %copy.11), channel_id=1, source_target_pairs={{0,4},{4,8},{8,12},{12,16},{16,20},{20,24},{24,28},{28,0},{1,5},{5... | collective-permute-start | bytes 6291464 | tf_op jit(solution)/shard_map/ppermute | solution.py:38
  13.2 92.4 %collective-permute-start.1 = (bf16[128,8192]{0,1:T(8,128)(2,1)S(1)}, bf16[128,8192]{0,1:T(8,128)(2,1)}, u32[]{:S(2)}, u32[]{:S(2)}) collective-permute-start(bf16[128,8192]{0,1:T(8,128)(2,1)S(1)} %copy.11), channel_id=1, source_target_pairs={{0,28},{4,0},{8,4},{12,8},{16,12},{20,16},{24,20},{28,24},{1,29},{... | collective-permute-start | bytes 6291464 | tf_op jit(solution)/shard_map/ppermute | solution.py:43
  103.1 91.9 %collective-permute-start.2 = (bf16[128,8192]{0,1:T(8,128)(2,1)}, bf16[128,8192]{0,1:T(8,128)(2,1)}, u32[]{:S(2)}, u32[]{:S(2)}) collective-permute-start(bf16[128,8192]{0,1:T(8,128)(2,1)} %collective-permute-done), channel_id=1, source_target_pairs={{0,4},{4,8},{8,12},{12,16},{16,20},{20,24},{24,28},{28,0},{1,5},{5... | collective-permute-start | bytes 6291464 | tf_op jit(solution)/shard_map/ppermute | solution.py:38
  105.7 97.8 %collective-permute-start.3 = (bf16[128,8192]{0,1:T(8,128)(2,1)}, bf16[128,8192]{0,1:T(8,128)(2,1)}, u32[]{:S(2)}, u32[]{:S(2)}) collective-permute-start(bf16[128,8192]{0,1:T(8,128)(2,1)} %collective-permute-done.1), channel_id=1, source_target_pairs={{0,28},{4,0},{8,4},{12,8},{16,12},{20,16},{24,20},{28,24},{1,29},{... | collective-permute-start | bytes 6291464 | tf_op jit(solution)/shard_map/ppermute | solution.py:43
  114.7 1.5 copy-start.3
  194.9 91.1 %collective-permute-start.4 = (bf16[128,8192]{0,1:T(8,128)(2,1)}, bf16[128,8192]{0,1:T(8,128)(2,1)S(1)}, u32[]{:S(2)}, u32[]{:S(2)}) collective-permute-start(bf16[128,8192]{0,1:T(8,128)(2,1)} %collective-permute-done.2), channel_id=1, source_target_pairs={{0,4},{4,8},{8,12},{12,16},{16,20},{20,24},{24,28},{28,0},{1,5},{5... | collective-permute-start | bytes 6291464 | tf_op jit(solution)/shard_map/ppermute | solution.py:38
  203.5 130.9 %collective-permute-start.5 = (bf16[128,8192]{0,1:T(8,128)(2,1)}, bf16[128,8192]{0,1:T(8,128)(2,1)S(1)}, u32[]{:S(2)}, u32[]{:S(2)}) collective-permute-start(bf16[128,8192]{0,1:T(8,128)(2,1)} %collective-permute-done.3), channel_id=1, source_target_pairs={{0,28},{4,0},{8,4},{12,8},{16,12},{20,16},{24,20},{28,24},{1,29},{... | collective-permute-start | bytes 6291464 | tf_op jit(solution)/shard_map/ppermute | solution.py:43
  286.0 49.9 %collective-permute-start.6 = (bf16[128,8192]{0,1:T(8,128)(2,1)S(1)}, bf16[128,8192]{0,1:T(8,128)(2,1)S(1)}, u32[]{:S(2)}, u32[]{:S(2)}) collective-permute-start(bf16[128,8192]{0,1:T(8,128)(2,1)S(1)} %collective-permute-done.4), channel_id=1, source_target_pairs={{0,4},{4,8},{8,12},{12,16},{16,20},{20,24},{24,28},{28,0},{1,5},{5... | collective-permute-start | bytes 6291464 | tf_op jit(solution)/shard_map/ppermute | solution.py:38
  526.1 13.2 %copy-start.1 = (f32[4096]{0:T(1024)S(1)}, f32[4096]{0:T(1024)}, u32[]{:S(2)}) copy-start(f32[4096]{0:T(1024)} %param.12) | copy-start | bytes 49156
  526.1 13.2 %copy-start.2 = (f32[4096]{0:T(1024)S(1)}, f32[4096]{0:T(1024)}, u32[]{:S(2)}) copy-start(f32[4096]{0:T(1024)} %param.13) | copy-start | bytes 49156
  543.8 105.8 %all-reduce.2.cloned.1.call-start = ((), (), s32[]{:S(2)}) async-start(), calls=%async_computation.1 | async-start | bytes 524288 | tf_op jit(solution)/shard_map/psum | solution.py:58
  579.0 131.1 %all-gather.5.cloned.1.call-start = ((), (), s32[]{:S(2)}) async-start(), calls=%async_computation.2 | async-start | bytes 10485760 | tf_op jit(solution)/shard_map/all_gather | solution.py:64
Sparse Core Ops, SparseCore 0:
  544.0 31.2 all-gather.2
  579.1 70.5 all-reduce.1
  651.3 58.6 all-gather.4
